TPU v7x, 128 devices: a whole 4x4x4 slice. The times are simulated.
128 devices in a mesh: rep: 4 (over y), shard: 32 (over x, z, core).
Axes of the slice: x: 4, y: 4, z: 4, core: 2. Of those that a mesh axis runs over, the one named last changes fastest.
Arguments:
- embed_table: bfloat16 [262144, 128], P('shard'), may hold values from -6 to 6
- row_ids: int32 [128, 8192], P(('rep', 'shard')), may hold values from 0 to 1023
- row_owner: int32 [128, 8192, 1], P(('rep', 'shard')), may hold values from 0 to 31; in each aligned block of 8192 rows (0 to 8191, 8192 to 16383, ..., all dimensions but the last counted through in order) at most 512 rows name the same one
- lengths: int32 [128, 1024], P(('rep', 'shard')), may hold values from 1 to 200, 8192 in all within a row
- feature_slot: int32 [32, 8], replicated, may hold values from 0 to 7, each once within a row
- labels: int32 [16384], P(('rep', 'shard')), may hold values 0 or 1
- norm_gain: float32 [1024], replicated, may hold values from 0.1 to 1.9
- cross_weight: bfloat16 [3, 1024, 1024], replicated, may hold values from -0.1875 to 0.1875
- cross_bias: float32 [3, 1024], replicated, may hold values from -3 to 3
- deep_weight: bfloat16 [3, 1024, 1024], replicated, may hold values from -0.1875 to 0.1875
- deep_bias: float32 [3, 1024], replicated, may hold values from -3 to 3
- out_weight: float32 [1024], replicated, may hold values from -0.1875 to 0.1875
Outputs:
- row_grad: float32 [262144, 128], P('shard')
- first_grad: float32 [1024, 1024], replicated
- logits: float32 [16384], P(('rep', 'shard'))
Inputs may be any that keep to these rules, and one draw needn't show every extreme that they name: `row_owner`: among one device's ids, at most 512 have the same owner, and in every draw some device sends exactly 512 to some owner. Each device's 1024 lengths sum to 8192; the largest is 200. `feature_slot`: each row holds each of 0 to 7 once.
All inputs are finite; a program needn't handle non-finite values. No bound on the sum of `labels` on one device may be relied on, other than what follows from the above.
Results may differ from a plain program's by a relative error of at most 0.035.
Values may be sent and summed in bfloat16 or wider, within the bound.
No kernel may reach another device: no remote copies, remote signals or barrier semaphores. Data moves between devices by JAX's collectives and lax.ppermute only.
A program may use at most 128 MiB of HBM per device.

v0:
```python
import jax
import jax.numpy as jnp
from jax import lax
from jax.sharding import PartitionSpec as P


def times_transposed(left, right):
    return lax.dot_general(
        left, right, (((1,), (1,)), ((), ())), preferred_element_type=jnp.float32
    )


def forward_backward(
    pooled, labels, norm_gain, cross_weight, cross_bias, deep_weight, deep_bias, out_weight
):
    mean_square = jnp.mean(pooled * pooled, axis=1, keepdims=True)
    inverse = lax.rsqrt(mean_square + 1e-06)
    start_row = (pooled * inverse * norm_gain).astype(jnp.bfloat16)
    start_float = start_row.astype(jnp.float32)
    current = start_row
    cross_terms = []
    for layer_number in range(cross_weight.shape[0]):
        product = (
            jnp.dot(current, cross_weight[layer_number], preferred_element_type=jnp.float32)
            + cross_bias[layer_number]
        )
        cross_terms.append(product)
        current = (start_float * product + current.astype(jnp.float32)).astype(jnp.bfloat16)
    deep_terms = []
    for layer_number in range(deep_weight.shape[0]):
        product = (
            jnp.dot(current, deep_weight[layer_number], preferred_element_type=jnp.float32)
            + deep_bias[layer_number]
        )
        deep_terms.append(product)
        current = (product * jax.nn.sigmoid(product)).astype(jnp.bfloat16)
    logits = jnp.sum(current.astype(jnp.float32) * out_weight, axis=1)
    error = jax.nn.sigmoid(logits) - labels.astype(jnp.float32)
    grad = error[:, None] * out_weight[None, :]
    for layer_number in reversed(range(deep_weight.shape[0])):
        product = deep_terms[layer_number]
        sig = jax.nn.sigmoid(product)
        masked = (grad * sig * (1.0 + product * (1.0 - sig))).astype(jnp.bfloat16)
        grad = times_transposed(masked, deep_weight[layer_number])
    grad_start = jnp.zeros_like(grad)
    first_grad = jnp.zeros((start_row.shape[1], start_row.shape[1]), jnp.float32)
    for layer_number in reversed(range(cross_weight.shape[0])):
        grad_cross = (grad * start_float).astype(jnp.bfloat16)
        grad_start = grad_start + grad * cross_terms[layer_number]
        if layer_number == 0:
            first_grad = lax.dot_general(
                start_row, grad_cross, (((0,), (0,)), ((), ())), preferred_element_type=jnp.float32
            )
        grad = grad + times_transposed(grad_cross, cross_weight[layer_number])
    grad_start = grad_start + grad
    scaled = grad_start * norm_gain
    grad_pooled = inverse * scaled - pooled * inverse**3 * jnp.mean(
        scaled * pooled, axis=1, keepdims=True
    )
    return (logits, grad_pooled.astype(jnp.bfloat16), first_grad)


def body(
    embed_table,
    row_ids,
    row_owner,
    lengths,
    feature_slot,
    labels,
    norm_gain,
    cross_weight,
    cross_bias,
    deep_weight,
    deep_bias,
    out_weight,
):
    shards = lax.axis_size("shard")
    id_count = row_ids.shape[1]
    bag_count = lengths.shape[1]
    features = feature_slot.shape[1]
    rows_local = embed_table.shape[0]
    width = embed_table.shape[1]
    capacity = 2 * id_count // shards
    vocab = rows_local // features
    ends = jnp.cumsum(lengths[0], dtype=jnp.int32)
    positions = jnp.arange(id_count, dtype=jnp.int32)
    bag_index = jnp.searchsorted(ends, positions, side="right")
    feature_of = bag_index % features
    owners = row_owner[0, :, 0]
    slot_base = feature_slot.reshape(-1)[owners * features + feature_of]
    local_row = slot_base * vocab + row_ids[0]
    matches = (owners[:, None] == jnp.arange(shards, dtype=jnp.int32)[None, :]).astype(jnp.int32)
    rank = jnp.sum(jnp.cumsum(matches, axis=0) * matches, axis=1) - 1
    slot = owners * capacity + rank
    row_send = (
        jnp.zeros((shards * capacity,), jnp.int32).at[slot].set(local_row).reshape(shards, capacity)
    )
    bag_send = (
        jnp.full((shards * capacity,), -1, jnp.int32)
        .at[slot]
        .set(bag_index)
        .reshape(shards, capacity)
    )
    row_recv, bag_recv = (
        lax.all_to_all(row_send, "shard", split_axis=0, concat_axis=0, tiled=True),
        lax.all_to_all(bag_send, "shard", split_axis=0, concat_axis=0, tiled=True),
    )
    filled = bag_recv >= 0
    looked = jnp.where(filled[:, :, None], embed_table[row_recv], jnp.zeros((), jnp.bfloat16))
    source_bag = (
        jnp.arange(shards, dtype=jnp.int32)[:, None] * bag_count + jnp.maximum(bag_recv, 0)
    ).reshape(-1)
    earlier = jnp.concatenate([jnp.full((shards, 1), -2, jnp.int32), bag_recv[:, :-1]], axis=1)
    run_start = filled & (bag_recv != earlier)
    slot_numbers = jnp.broadcast_to(
        jnp.arange(capacity, dtype=jnp.int32)[None, :], (shards, capacity)
    )
    first_slot = lax.cummax(jnp.where(run_start, slot_numbers, 0), axis=1)
    target = (jnp.arange(shards, dtype=jnp.int32)[:, None] * capacity + first_slot).reshape(-1)
    slot_sums = jax.ops.segment_sum(
        looked.reshape(-1, width).astype(jnp.float32), target, num_segments=shards * capacity
    )
    returned = lax.all_to_all(
        slot_sums.reshape(shards, capacity, width), "shard", split_axis=0, concat_axis=0, tiled=True
    )
    pooled = jax.ops.segment_sum(
        returned.reshape(-1, width), jnp.maximum(bag_send, 0).reshape(-1), num_segments=bag_count
    )
    samples = bag_count // features
    logits, grad_pooled, first_local = forward_backward(
        pooled.reshape(samples, features * width),
        labels,
        norm_gain,
        cross_weight,
        cross_bias,
        deep_weight,
        deep_bias,
        out_weight,
    )
    list_grads = grad_pooled.reshape(bag_count, width)
    everyone = lax.all_gather(list_grads, "shard", axis=0, tiled=True)
    picked = everyone[source_bag].reshape(shards, capacity, width)
    slot_values = jnp.where(filled[:, :, None], picked, jnp.zeros((), jnp.bfloat16))
    local_grad = jax.ops.segment_sum(
        slot_values.reshape(-1, width).astype(jnp.float32),
        row_recv.reshape(-1),
        num_segments=rows_local,
    )
    row_grad = lax.psum(local_grad, "rep")
    first_grad = lax.psum(first_local, ("rep", "shard"))
    return (row_grad, first_grad, logits)


def solution(mesh):
    in_specs = (
        P("shard", None),
        P(("rep", "shard"), None),
        P(("rep", "shard"), None, None),
        P(("rep", "shard"), None),
        P(),
        P(("rep", "shard")),
        P(),
        P(),
        P(),
        P(),
        P(),
        P(),
    )
    out_specs = (P("shard", None), P(), P(("rep", "shard")))
    return jax.shard_map(body, mesh=mesh, in_specs=in_specs, out_specs=out_specs, check_vma=False)
```

profile of v0, /device:TPU:38, one launch (start us, length us, event | category | flops | bytes accessed | tf_op | source)
XLA Modules:
  0.0 1753.7 jit_solution(7038976364346138722)
XLA Ops:
  10.0 17.1 reduce-window.21
  30.1 362.8 %while.24 = (s32[]{:T(128)}, u32[8192]{0:T(1024)S(1)}, u32[8192]{0:T(1024)S(1)}, s32[1024]{0:T(1024)S(1)}, s32[]{:T(128)}, /*index=5*/s32[]{:T(128)}, s32[]{}) while((s32[]{:T(128)}, u32[8192]{0:T(1024)S(1)}, u32[8192]{0:T(1024)S(1)}, s32[1024]{0:T(1024)S(1)}, s32[]{:T(128)}, /*index=5*/s32[]{:T(128)}, s32[]{}) %tuple.44), condition=%wide.region_6.7_spmd.clone, body=%wide.region_5.6_spmd.clone.sunk | while | flops 155652 | bytes 508005 | solution.py:87
  30.1 32.9 %gather_fusion = s32[8192]{0:T(1024)S(1)} fusion(s32[1024]{0:T(1024)S(1)} %get-tuple-element.154, u32[8192]{0:T(1024)S(1)} %broadcast_clamp_fusion.4), kind=kCustom, calls=%fused_computation.clone.clone.1 | custom fusion | bytes 98304 | tf_op jit(solution)/shard_map/jit(searchsorted)/jit(_searchsorted_scan_impl)/vmap(jit(_searchsorted_scan_impl))/while/body/eval_jaxpr/gather | solution.py:87
  63.1 32.9 %gather_fusion = s32[8192]{0:T(1024)S(1)} fusion(s32[1024]{0:T(1024)S(1)} %get-tuple-element.154, u32[8192]{0:T(1024)S(1)} %broadcast_clamp_fusion.4), kind=kCustom, calls=%fused_computation.clone.clone.1 | custom fusion | bytes 98304 | tf_op jit(solution)/shard_map/jit(searchsorted)/jit(_searchsorted_scan_impl)/vmap(jit(_searchsorted_scan_impl))/while/body/eval_jaxpr/gather | solution.py:87
  96.1 32.9 %gather_fusion = s32[8192]{0:T(1024)S(1)} fusion(s32[1024]{0:T(1024)S(1)} %get-tuple-element.154, u32[8192]{0:T(1024)S(1)} %broadcast_clamp_fusion.4), kind=kCustom, calls=%fused_computation.clone.clone.1 | custom fusion | bytes 98304 | tf_op jit(solution)/shard_map/jit(searchsorted)/jit(_searchsorted_scan_impl)/vmap(jit(_searchsorted_scan_impl))/while/body/eval_jaxpr/gather | solution.py:87
  129.1 32.9 %gather_fusion = s32[8192]{0:T(1024)S(1)} fusion(s32[1024]{0:T(1024)S(1)} %get-tuple-element.154, u32[8192]{0:T(1024)S(1)} %broadcast_clamp_fusion.4), kind=kCustom, calls=%fused_computation.clone.clone.1 | custom fusion | bytes 98304 | tf_op jit(solution)/shard_map/jit(searchsorted)/jit(_searchsorted_scan_impl)/vmap(jit(_searchsorted_scan_impl))/while/body/eval_jaxpr/gather | solution.py:87
  162.1 32.9 %gather_fusion = s32[8192]{0:T(1024)S(1)} fusion(s32[1024]{0:T(1024)S(1)} %get-tuple-element.154, u32[8192]{0:T(1024)S(1)} %broadcast_clamp_fusion.4), kind=kCustom, calls=%fused_computation.clone.clone.1 | custom fusion | bytes 98304 | tf_op jit(solution)/shard_map/jit(searchsorted)/jit(_searchsorted_scan_impl)/vmap(jit(_searchsorted_scan_impl))/while/body/eval_jaxpr/gather | solution.py:87
  195.0 32.9 %gather_fusion = s32[8192]{0:T(1024)S(1)} fusion(s32[1024]{0:T(1024)S(1)} %get-tuple-element.154, u32[8192]{0:T(1024)S(1)} %broadcast_clamp_fusion.4), kind=kCustom, calls=%fused_computation.clone.clone.1 | custom fusion | bytes 98304 | tf_op jit(solution)/shard_map/jit(searchsorted)/jit(_searchsorted_scan_impl)/vmap(jit(_searchsorted_scan_impl))/while/body/eval_jaxpr/gather | solution.py:87
  228.0 32.9 %gather_fusion = s32[8192]{0:T(1024)S(1)} fusion(s32[1024]{0:T(1024)S(1)} %get-tuple-element.154, u32[8192]{0:T(1024)S(1)} %broadcast_clamp_fusion.4), kind=kCustom, calls=%fused_computation.clone.clone.1 | custom fusion | bytes 98304 | tf_op jit(solution)/shard_map/jit(searchsorted)/jit(_searchsorted_scan_impl)/vmap(jit(_searchsorted_scan_impl))/while/body/eval_jaxpr/gather | solution.py:87
  261.0 32.9 %gather_fusion = s32[8192]{0:T(1024)S(1)} fusion(s32[1024]{0:T(1024)S(1)} %get-tuple-element.154, u32[8192]{0:T(1024)S(1)} %broadcast_clamp_fusion.4), kind=kCustom, calls=%fused_computation.clone.clone.1 | custom fusion | bytes 98304 | tf_op jit(solution)/shard_map/jit(searchsorted)/jit(_searchsorted_scan_impl)/vmap(jit(_searchsorted_scan_impl))/while/body/eval_jaxpr/gather | solution.py:87
  294.0 32.9 %gather_fusion = s32[8192]{0:T(1024)S(1)} fusion(s32[1024]{0:T(1024)S(1)} %get-tuple-element.154, u32[8192]{0:T(1024)S(1)} %broadcast_clamp_fusion.4), kind=kCustom, calls=%fused_computation.clone.clone.1 | custom fusion | bytes 98304 | tf_op jit(solution)/shard_map/jit(searchsorted)/jit(_searchsorted_scan_impl)/vmap(jit(_searchsorted_scan_impl))/while/body/eval_jaxpr/gather | solution.py:87
  327.0 32.9 %gather_fusion = s32[8192]{0:T(1024)S(1)} fusion(s32[1024]{0:T(1024)S(1)} %get-tuple-element.154, u32[8192]{0:T(1024)S(1)} %broadcast_clamp_fusion.4), kind=kCustom, calls=%fused_computation.clone.clone.1 | custom fusion | bytes 98304 | tf_op jit(solution)/shard_map/jit(searchsorted)/jit(_searchsorted_scan_impl)/vmap(jit(_searchsorted_scan_impl))/while/body/eval_jaxpr/gather | solution.py:87
  360.0 32.9 %gather_fusion = s32[8192]{0:T(1024)S(1)} fusion(s32[1024]{0:T(1024)S(1)} %get-tuple-element.154, u32[8192]{0:T(1024)S(1)} %broadcast_clamp_fusion.4), kind=kCustom, calls=%fused_computation.clone.clone.1 | custom fusion | bytes 98304 | tf_op jit(solution)/shard_map/jit(searchsorted)/jit(_searchsorted_scan_impl)/vmap(jit(_searchsorted_scan_impl))/while/body/eval_jaxpr/gather | solution.py:87
  392.9 31.0 %scatter_custom_fusion.1 = s32[16384]{0:T(1024)} fusion(s32[8192]{0:T(1024)S(1)} %bitcast.171, s32[8192]{0:T(1024)S(1)} %convert_element_type.85, s32[]{:T(128)} %constant.80.clone.1), kind=kCustom, calls=%fused_computation.152 | custom fusion | bytes 65540 | tf_op jit(solution)/shard_map/scatter | solution.py:101
  424.0 8.0 all-to-all-start.1
  432.2 51.0 %gather_fusion.1 = s32[8192]{0:T(1024)S(1)} fusion(s32[256]{0:T(256)S(1)} %reshape.250, s32[8192]{0:T(1024)S(1)} %fusion.139), kind=kCustom, calls=%fused_computation.1 | custom fusion | bytes 98304 | tf_op jit(solution)/shard_map/gather | solution.py:90
  483.4 31.0 %scatter_custom_fusion = s32[16384]{0:T(1024)} fusion(s32[8192]{0:T(1024)S(1)} %bitcast.172, s32[8192]{0:T(1024)S(1)} %multiply_add_fusion, s32[]{:T(128)} %constant.78.clone.1), kind=kCustom, calls=%fused_computation.156 | custom fusion | bytes 65540 | tf_op jit(solution)/shard_map/scatter | solution.py:96
  526.7 156.0 %scatter_custom_fusion.2 = f32[16384,128]{1,0:T(8,128)} fusion(s32[16384]{0:T(1024)S(1)} %bitcast.167, f32[]{:T(128)} %constant.77.clone.1, pred[16384]{0:T(1024)(128)(4,1)S(1)} %bitcast.163, bf16[]{:T(256)} %constant.91.clone.1, bf16[8192,128]{1,0:T(8,128)(2,1)S(1)} %copy-done, s32[16384]{0:T(1024)S(1)} %broadcast_clamp_fusion.2), kind=kCustom, calls=%fused_computation.17 | custom fusion | flops 6291456 | bytes 10567686 | tf_op jit(solution)/shard_map/scatter-add | solution.py:120
  682.7 20.0 %all-to-all-start.2 = ((f32[32,512,128]{2,1,0:T(8,128)}), f32[32,512,128]{2,1,0:T(8,128)}, u32[]{:S(2)}, u32[]{:S(2)}) async-start(f32[32,512,128]{2,1,0:T(8,128)} %bitcast.148), calls=%async_computation.2 | async-start | bytes 16777216 | tf_op jit(solution)/shard_map/all_to_all | solution.py:123
  704.9 109.2 %all-to-all-done.2 = f32[32,512,128]{2,1,0:T(8,128)} async-done(((f32[32,512,128]{2,1,0:T(8,128)}), f32[32,512,128]{2,1,0:T(8,128)}, u32[]{:S(2)}, u32[]{:S(2)}) %all-to-all-start.2) | async-done | bytes 8388640 | tf_op jit(solution)/shard_map/all_to_all | solution.py:123
  814.1 100.9 %scatter_custom_fusion.3 = f32[1024,128]{1,0:T(8,128)S(1)} fusion(s32[16384]{0:T(1024)S(1)} %broadcast_maximum_fusion.2, f32[16384,128]{1,0:T(8,128)} %bitcast.17, f32[]{:T(128)} %constant.77.clone.1), kind=kCustom, calls=%fused_computation.128 | custom fusion | flops 2097152 | bytes 524800 | tf_op jit(solution)/shard_map/scatter-add | solution.py:126
  953.8 61.9 %all-gather.2.cloned.1.call-done = bf16[32768,128]{1,0:T(8,128)(2,1)} async-done(((bf16[1024,128]{1,0:T(8,128)(2,1)}), bf16[32768,128]{1,0:T(8,128)(2,1)}) %all-gather.2.cloned.1.call-update) | async-done | bytes 8388624 | tf_op jit(solution)/shard_map/all_gather | solution.py:141
  1015.8 316.6 %scatter_custom_fusion.4 = f32[8192,128]{1,0:T(8,128)} fusion(s32[16384]{0:T(1024)S(1)} %bitcast.161, pred[16384]{0:T(1024)(128)(4,1)S(1)} %bitcast.164, bf16[]{:T(256)} %constant.91.clone.1, f32[]{:T(128)} %constant.77.clone.1, bf16[32768,128]{1,0:T(8,128)(2,1)} %all-gather.2.cloned.1.call-done, s32[16384]{0:T(1024)S(1)} %broadcast_clamp_fusion.1), kind=kCustom, calls=%fused_computation.15 | custom fusion | flops 6291456 | bytes 12664838 | tf_op jit(solution)/shard_map/scatter-add | solution.py:144
  1332.5 407.2 %all-reduce.4.cloned.1.call-done = f32[8192,128]{1,0:T(8,128)} async-done(((f32[8192,128]{1,0:T(8,128)}), f32[8192,128]{1,0:T(8,128)}) %all-reduce.4.cloned.1.call-update) | async-done | bytes 4194320 | tf_op jit(solution)/shard_map/psum | solution.py:149
  (181 shorter events, 65.2 us)
Async XLA Ops:
  8.0 518.7 %copy-start = (bf16[8192,128]{1,0:T(8,128)(2,1)S(1)}, bf16[8192,128]{1,0:T(8,128)(2,1)}, u32[]{:S(2)}) copy-start(bf16[8192,128]{1,0:T(8,128)(2,1)} %param.14) | copy-start | bytes 6291460
  8.0 20.6 %copy-start.8 = (s32[1,8192,1]{1,2,0:T(1,128)S(1)}, s32[1,8192,1]{1,2,0:T(1,128)}, u32[]{:S(2)}) copy-start(s32[1,8192,1]{1,2,0:T(1,128)} %param.16) | copy-start | bytes 98308
  8.0 21.5 %copy-start.17 = (s32[1,1024]{1,0:T(1,128)S(1)}, s32[1,1024]{1,0:T(1,128)}, u32[]{:S(2)}) copy-start(s32[1,1024]{1,0:T(1,128)} %param.17) | copy-start | bytes 12292
  30.1 401.9 %copy-start.16 = (s32[32,8]{0,1:T(8,128)S(1)}, s32[32,8]{0,1:T(8,128)}, u32[]{:S(2)}) copy-start(s32[32,8]{0,1:T(8,128)} %param.18) | copy-start | bytes 3076
  424.0 90.4 %all-to-all-start.1 = ((s32[32,1,512]{2,1,0:T(1,128)}), s32[32,1,512]{2,1,0:T(1,128)S(1)}, u32[]{:S(2)}, u32[]{:S(2)}) async-start(s32[32,1,512]{2,1,0:T(1,128)} %bitcast.11), calls=%async_computation.1 | async-start | bytes 131072 | tf_op jit(solution)/shard_map/all_to_all | solution.py:106
  432.2 51.0 %copy-start.10 = (s32[1,8192]{1,0:T(1,128)S(1)}, s32[1,8192]{1,0:T(1,128)}, u32[]{:S(2)}) copy-start(s32[1,8192]{1,0:T(1,128)} %param.15) | copy-start | bytes 98308
  514.4 12.1 all-to-all-start
  682.7 20.1 %copy-start.12 = (f32[3,1024]{1,0:T(4,128)S(1)}, f32[3,1024]{1,0:T(4,128)}, u32[]{:S(2)}) copy-start(f32[3,1024]{1,0:T(4,128)} %param.22) | copy-start | bytes 36868
  682.7 20.7 %copy-start.13 = (f32[3,1024]{1,0:T(4,128)S(1)}, f32[3,1024]{1,0:T(4,128)}, u32[]{:S(2)}) copy-start(f32[3,1024]{1,0:T(4,128)} %param.24) | copy-start | bytes 36868
  682.7 131.3 %all-to-all-start.2 = ((f32[32,512,128]{2,1,0:T(8,128)}), f32[32,512,128]{2,1,0:T(8,128)}, u32[]{:S(2)}, u32[]{:S(2)}) async-start(f32[32,512,128]{2,1,0:T(8,128)} %bitcast.148), calls=%async_computation.2 | async-start | bytes 16777216 | tf_op jit(solution)/shard_map/all_to_all | solution.py:123
  702.7 313.0 %all-gather.2.cloned.1.call-start = ((), (), s32[]{:S(2)}) async-start(), calls=%async_computation.3 | async-start | bytes 8650752 | tf_op jit(solution)/shard_map/all_gather | solution.py:141
  923.5 4.6 copy-start.11
  923.5 6.9 slice-start
  925.7 4.7 copy-start.1
  925.7 4.7 slice-start.1
  925.7 4.7 copy-start.19
  937.9 7.5 copy-start.2
  937.9 7.5 copy-start.4
  937.9 7.5 copy-start.9
  943.0 5.3 copy-start.15
  943.0 5.3 copy-start.20
  949.3 383.1 %all-reduce.6.cloned.1.call-start = ((), (), s32[]{:S(2)}) async-start(), calls=%async_computation.5 | async-start | bytes 8388608 | tf_op jit(solution)/shard_map/psum | solution.py:150
  953.4 786.2 %all-reduce.4.cloned.1.call-start = ((), (), s32[]{:S(2)}) async-start(), calls=%async_computation.4 | async-start | bytes 8388608 | tf_op jit(solution)/shard_map/psum | solution.py:149
  1739.7 4.6 copy-start.6
  (9 other events, 18.0 us)
Sparse Core Ops, SparseCore 0:
  949.4 66.2 all-gather.1
Sparse Core Ops, SparseCore 1:
  955.3 176.9 all-reduce.5
  1332.5 407.1 all-reduce.3
where the time goes:
time: 1760 us; the launch traced here: 1750 us
  other arithmetic  602 us (34%)
  waiting for transfers between devices  581 us (33%)
  local copies, waits for them, and re-layouts  489 us (28%)
  starting transfers between devices  35.7 us (2%)
  matrix products  29.6 us (2%)
    psum x1, waiting for transfers between devices, body(): row_grad = lax.psum(local_grad, 'rep')  407 us
    gather x11, local copies, waits for them, and re-layouts, body(): bag_index = jnp.searchsorted(ends, positions, side='right')  362 us
    scatter-add x1, other arithmetic, body(): jax.ops.segment_sum(slot_values.reshape(-1, width).astype(jnp.float32), r...  317 us
    scatter-add x1, other arithmetic, body(): jax.ops.segment_sum(looked.reshape(-1, width).astype(jnp.float32), target...  156 us
    all_to_all x1, waiting for transfers between devices, body(): lax.all_to_all(slot_sums.reshape(shards, capacity, width), 'shard', split...  109 us
    scatter-add x1, other arithmetic, body(): jax.ops.segment_sum(returned.reshape(-1, width), jnp.maximum(bag_send, 0)...  101 us
    all_gather x1, waiting for transfers between devices, body(): everyone = lax.all_gather(list_grads, 'shard', axis=0, tiled=True)  61.9 us
    gather x1, local copies, waits for them, and re-layouts, body(): slot_base = feature_slot.reshape(-1)[owners * features + feature_of]  51 us
  transfers between devices with their start and end apart: 6, of which 4 were waited for; matrix products, arithmetic and copies ran while one was open for 23% of the time, Pallas kernels for 0%

commit v1 on v0

v1 whole, which is shorter than its diff:
```python
import functools

import jax
import jax.numpy as jnp
import numpy as np
from jax import lax
from jax.experimental import pallas as pl
from jax.experimental.pallas import tpu as pltpu
from jax.sharding import PartitionSpec as P

BF = jnp.bfloat16
F32 = jnp.float32
I32 = jnp.int32
OWNERS = 32
FEATS = 8
KEYS = OWNERS * FEATS
CAP = 512
VOC = 1024
ROWS = FEATS * VOC
EMB = 128
BAGS = 1024
SAMPLES = 128
WIDTH = FEATS * EMB
IDS = 8192
REPS = 4
PAIR = FEATS // REPS
LANES = 256
IDROWS = IDS // LANES
ACCS = 8
VMEM = 56 * 1024 * 1024

NT = (((1,), (1,)), ((), ()))
TN = (((0,), (0,)), ((), ()))


def dot(a, b, dims=(((1,), (0,)), ((), ()))):
    return lax.dot_general(a, b, dims, preferred_element_type=F32)


def iota(shape, dim):
    return lax.broadcasted_iota(I32, shape, dim)


def onehot(cond):
    return jnp.where(cond, 1.0, 0.0).astype(BF)


def index_kernel(ids_ref, owner_ref, len_ref, slot_ref, out_ref, bag_ref, key_ref):
    lens = len_ref[...].astype(F32).astype(BF)
    incl128 = onehot(iota((128, 128), 0) <= iota((128, 128), 1))
    within = dot(lens, incl128)
    total = jnp.broadcast_to(within[:, 127:128], (8, 128))
    high = jnp.floor(total * (1.0 / 256.0))
    low = total - high * 256.0
    below8 = onehot(iota((8, 8), 1) < iota((8, 8), 0))
    before = dot(below8, high.astype(BF)) * 256.0 + dot(below8, low.astype(BF))
    start = (within + before).astype(I32) - len_ref[...]
    start_hi = start >> 8
    start_lo = start & 255
    marks = jnp.zeros((IDROWS, LANES), F32)
    for r in range(8):
        a = onehot(iota((IDROWS, 128), 0) == start_hi[r : r + 1, :])
        b = onehot(iota((LANES, 128), 0) == start_lo[r : r + 1, :])
        marks = marks + dot(a, b, NT)
    marks = marks.astype(BF)
    incl = onehot(iota((LANES, LANES), 0) <= iota((LANES, LANES), 1))
    strict = onehot(iota((LANES, LANES), 0) < iota((LANES, LANES), 1))
    row_counts = dot(marks, jnp.ones((LANES, LANES), BF))
    below = onehot(iota((IDROWS, IDROWS), 1) < iota((IDROWS, IDROWS), 0))
    bag = (dot(marks, incl) + dot(below, row_counts.astype(BF))).astype(I32) - 1
    bag_ref[...] = bag
    key_ref[...] = owner_ref[...] * FEATS + (bag & (FEATS - 1))

    key_iota = iota((KEYS, LANES), 0)

    def count(r, acc):
        return acc + jnp.where(key_iota == key_ref[pl.ds(r, 1), :], 1.0, 0.0)

    counts = lax.fori_loop(0, IDROWS, count, jnp.zeros((KEYS, LANES), F32))
    totals = dot(counts.astype(BF), jnp.ones((LANES, LANES), BF))
    high = jnp.floor(totals * (1.0 / 256.0))
    low = totals - high * 256.0
    ki, kj = iota((KEYS, KEYS), 0), iota((KEYS, KEYS), 1)
    earlier = onehot((ki // FEATS == kj // FEATS) & (kj < ki))
    carry0 = dot(earlier, high.astype(BF)) * 256.0 + dot(earlier, low.astype(BF))

    rank_iota = iota((CAP, LANES), 0)
    owner_iota = iota((OWNERS, LANES), 0)
    slots = jnp.broadcast_to(slot_ref[...].astype(F32), (KEYS, LANES))

    def place(r, state):
        carry, acc = state
        same = key_iota == key_ref[pl.ds(r, 1), :]
        hot = jnp.where(same, 1.0, 0.0)
        prefix = dot(hot.astype(BF), strict)
        rank = jnp.sum(jnp.where(same, prefix + carry, 0.0), axis=0, keepdims=True)
        slot = jnp.sum(jnp.where(same, slots, 0.0), axis=0, keepdims=True)
        rank = rank.astype(I32)
        row = slot.astype(I32) * VOC + ids_ref[pl.ds(r, 1), :]
        value = (1 << 23) + (row << 10) + bag_ref[pl.ds(r, 1), :]
        mine = owner_iota == owner_ref[pl.ds(r, 1), :]
        pieces = [
            jnp.where(mine, jnp.broadcast_to(p.astype(F32), (OWNERS, LANES)), 0.0)
            for p in (value & 255, (value >> 8) & 255, value >> 16)
        ]
        left = jnp.concatenate(pieces, axis=0).astype(BF)
        right = onehot(rank_iota == rank)
        acc = acc + dot(left, right, NT)
        carry = carry + jnp.sum(hot, axis=1, keepdims=True)
        return carry, acc

    _, acc = lax.fori_loop(
        0, IDROWS, place, (carry0, jnp.zeros((3 * OWNERS, CAP), F32))
    )
    acc = acc.astype(I32)
    out_ref[...] = (
        acc[:OWNERS] + (acc[OWNERS : 2 * OWNERS] << 8) + (acc[2 * OWNERS :] << 16)
    )


def index_call(ids, owners, lengths, slots):
    return pl.pallas_call(
        index_kernel,
        out_shape=jax.ShapeDtypeStruct((OWNERS, CAP), I32),
        scratch_shapes=[pltpu.VMEM((IDROWS, LANES), I32), pltpu.VMEM((IDROWS, LANES), I32)],
        compiler_params=pltpu.CompilerParams(vmem_limit_bytes=VMEM),
        name="index",
    )(ids, owners, lengths, slots)


def gather_kernel(row_ref, table_ref, out_ref, wide, picked):
    step = pl.program_id(0)

    @pl.when(step == 0)
    def _():
        wide[...] = table_ref[...].astype(F32)

    base = step * CAP

    def some(i, _):
        at = i * 16
        for j in range(16):
            row = row_ref[base + at + j]
            picked[pl.ds(at + j, 1), :] = wide[pl.ds(row, 1), :]
        return 0

    lax.fori_loop(0, CAP // 16, some, 0)
    out_ref[0] = picked[...].astype(BF)


def gather_call(rows, table):
    return pl.pallas_call(
        gather_kernel,
        out_shape=jax.ShapeDtypeStruct((OWNERS, CAP, EMB), BF),
        grid_spec=pltpu.PrefetchScalarGridSpec(
            num_scalar_prefetch=1,
            grid=(OWNERS,),
            in_specs=[pl.BlockSpec((ROWS, EMB), lambda i, r: (0, 0))],
            out_specs=pl.BlockSpec((1, CAP, EMB), lambda i, r: (i, 0, 0)),
            scratch_shapes=[pltpu.VMEM((ROWS, EMB), F32), pltpu.VMEM((CAP, EMB), F32)],
        ),
        compiler_params=pltpu.CompilerParams(vmem_limit_bytes=VMEM),
        name="gather",
    )(rows, table)


def sigmoid(x):
    return 1.0 / (1.0 + jnp.exp(-x))


def tower_kernel(
    got_ref,
    packed_ref,
    labels_ref,
    gain_ref,
    cbias_ref,
    dbias_ref,
    out_w_ref,
    cross_hbm,
    deep_hbm,
    logits_ref,
    grads_ref,
    first_ref,
    pooled_ref,
    cross_w,
    deep_w,
    start_ref,
    cross_t,
    deep_t,
    gx_ref,
    sems,
):
    step = pl.program_id(0)

    def copies():
        out = []
        for layer in range(3):
            out.append(
                pltpu.make_async_copy(cross_hbm.at[layer], cross_w.at[layer], sems.at[layer])
            )
            out.append(
                pltpu.make_async_copy(deep_hbm.at[layer], deep_w.at[layer], sems.at[3 + layer])
            )
        return out

    @pl.when(step == 0)
    def _():
        for copy in copies():
            copy.start()
        pooled_ref[...] = jnp.zeros_like(pooled_ref)

    packed = packed_ref[pl.ds(step, 1), :]
    bag = packed & (BAGS - 1)
    place = jnp.where(packed > 0, (bag & (FEATS - 1)) * SAMPLES + (bag >> 3), -1)
    hot = onehot(iota((BAGS, CAP), 0) == place)
    pooled_ref[...] += dot(hot, got_ref[0])

    @pl.when(step == OWNERS - 1)
    def _():
        for copy in copies():
            copy.wait()
        gain = gain_ref[...]
        pooled = jnp.concatenate(
            [pooled_ref[f * SAMPLES : (f + 1) * SAMPLES, :] for f in range(FEATS)], axis=1
        )
        inverse = lax.rsqrt(jnp.mean(pooled * pooled, axis=1, keepdims=True) + 1e-06)
        start = (pooled * inverse * gain).astype(BF)
        start_ref[...] = start
        current = start
        for layer in range(3):
            product = dot(current, cross_w[layer]) + cbias_ref[layer : layer + 1, :]
            cross_t[layer] = product
            current = (start_ref[...].astype(F32) * product + current.astype(F32)).astype(BF)
        for layer in range(3):
            product = dot(current, deep_w[layer]) + dbias_ref[layer : layer + 1, :]
            deep_t[layer] = product
            current = (product * sigmoid(product)).astype(BF)
        out_w = out_w_ref[...]
        logits = jnp.sum(current.astype(F32) * out_w, axis=1, keepdims=True)
        logits_ref[...] = logits
        error = sigmoid(logits) - labels_ref[...].astype(F32)
        grad = error * out_w
        for layer in (2, 1, 0):
            product = deep_t[layer]
            sig = sigmoid(product)
            masked = (grad * sig * (1.0 + product * (1.0 - sig))).astype(BF)
            grad = dot(masked, deep_w[layer], NT)
        gx_ref[...] = jnp.zeros_like(gx_ref)
        for layer in (2, 1, 0):
            crossed = (grad * start_ref[...].astype(F32)).astype(BF)
            gx_ref[...] += grad * cross_t[layer]
            grad = grad + dot(crossed, cross_w[layer], NT)
            if layer == 0:
                first_ref[...] = dot(start_ref[...], crossed, TN).astype(first_ref.dtype)
        scaled = (gx_ref[...] + grad) * gain
        pooled = jnp.concatenate(
            [pooled_ref[f * SAMPLES : (f + 1) * SAMPLES, :] for f in range(FEATS)], axis=1
        )
        inverse = lax.rsqrt(jnp.mean(pooled * pooled, axis=1, keepdims=True) + 1e-06)
        mean = jnp.mean(scaled * pooled, axis=1, keepdims=True)
        result = (inverse * scaled - pooled * (inverse * inverse * inverse) * mean).astype(BF)
        for r in range(REPS):
            grads_ref[r] = result[:, r * PAIR * EMB : (r + 1) * PAIR * EMB]


def tower_call(got, packed, labels, gain, cross, cbias, deep, dbias, out_w):
    def whole(shape):
        return pl.BlockSpec(shape, lambda i: (0,) * len(shape))

    return pl.pallas_call(
        tower_kernel,
        grid=(OWNERS,),
        in_specs=[
            pl.BlockSpec((1, CAP, EMB), lambda i: (i, 0, 0)),
            whole((OWNERS, CAP)),
            whole((SAMPLES, 1)),
            whole((1, WIDTH)),
            whole((3, WIDTH)),
            whole((3, WIDTH)),
            whole((1, WIDTH)),
            pl.BlockSpec(memory_space=pl.ANY),
            pl.BlockSpec(memory_space=pl.ANY),
        ],
        out_specs=[
            whole((SAMPLES, 1)),
            whole((REPS, SAMPLES, PAIR * EMB)),
            whole((WIDTH, WIDTH)),
        ],
        out_shape=[
            jax.ShapeDtypeStruct((SAMPLES, 1), F32),
            jax.ShapeDtypeStruct((REPS, SAMPLES, PAIR * EMB), BF),
            jax.ShapeDtypeStruct((WIDTH, WIDTH), BF),
        ],
        scratch_shapes=[
            pltpu.VMEM((BAGS, EMB), F32),
            pltpu.VMEM((3, WIDTH, WIDTH), BF),
            pltpu.VMEM((3, WIDTH, WIDTH), BF),
            pltpu.VMEM((SAMPLES, WIDTH), BF),
            pltpu.VMEM((3, SAMPLES, WIDTH), F32),
            pltpu.VMEM((3, SAMPLES, WIDTH), F32),
            pltpu.VMEM((SAMPLES, WIDTH), F32),
            pltpu.SemaphoreType.DMA((6,)),
        ],
        compiler_params=pltpu.CompilerParams(vmem_limit_bytes=VMEM),
        name="tower",
    )(got, packed, labels, gain, cbias, dbias, out_w, cross, deep)


def scatter_kernel(word_ref, first_ref, last_ref, grads_ref, out_ref, wide, *accs):
    step = pl.program_id(0)

    @pl.when(step == 0)
    def _():
        for acc in accs:
            acc[...] = jnp.zeros_like(acc)

    group = grads_ref.shape[0]
    for g in range(group):
        for r in range(REPS):
            block = grads_ref[g, r]
            base = (g * REPS + r) * PAIR * SAMPLES
            for f in range(PAIR):
                wide[base + f * SAMPLES : base + (f + 1) * SAMPLES, :] = block[
                    :, f * EMB : (f + 1) * EMB
                ].astype(F32)

    def device(k, _):
        base = k * (PAIR * SAMPLES)
        listed = (k & (REPS - 1)) * OWNERS + step * group + k // REPS

        def some(i, _):
            at = listed * CAP + i * ACCS
            for j in range(ACCS):
                word = word_ref[at + j]
                source = base + (word & 255)
                target = word >> 8
                acc = accs[j]
                acc[pl.ds(target, 1), :] += wide[pl.ds(source, 1), :]
            return 0

        lax.fori_loop(first_ref[listed], last_ref[listed], some, 0)
        return 0

    lax.fori_loop(0, group * REPS, device, 0)

    @pl.when(step == pl.num_programs(0) - 1)
    def _():
        total = accs[0][: PAIR * VOC, :]
        for acc in accs[1:]:
            total = total + acc[: PAIR * VOC, :]
        out_ref[...] = total.astype(out_ref.dtype)


def scatter_call(words, first, last, grads, group=2):
    rows = PAIR * VOC
    return pl.pallas_call(
        scatter_kernel,
        out_shape=jax.ShapeDtypeStruct((rows, EMB), BF),
        grid_spec=pltpu.PrefetchScalarGridSpec(
            num_scalar_prefetch=3,
            grid=(OWNERS // group,),
            in_specs=[
                pl.BlockSpec(
                    (group, REPS, SAMPLES, PAIR * EMB), lambda i, w, a, b: (i, 0, 0, 0)
                )
            ],
            out_specs=pl.BlockSpec((rows, EMB), lambda i, w, a, b: (0, 0)),
            scratch_shapes=[pltpu.VMEM((group * REPS * PAIR * SAMPLES, EMB), F32)]
            + [pltpu.VMEM((rows + 8, EMB), F32) for _ in range(ACCS)],
        ),
        compiler_params=pltpu.CompilerParams(vmem_limit_bytes=VMEM),
        name="scatter",
    )(words, first, last, grads)


def widen_kernel(order_ref, in_ref, out_ref):
    del order_ref
    out_ref[...] = in_ref[0].astype(F32)


def widen_call(order, blocks):
    return pl.pallas_call(
        widen_kernel,
        out_shape=jax.ShapeDtypeStruct((ROWS, EMB), F32),
        grid_spec=pltpu.PrefetchScalarGridSpec(
            num_scalar_prefetch=1,
            grid=(FEATS,),
            in_specs=[pl.BlockSpec((1, VOC, EMB), lambda i, o: (o[i], 0, 0))],
            out_specs=pl.BlockSpec((VOC, EMB), lambda i, o: (i, 0)),
        ),
        name="widen",
    )(order, blocks)


def body(
    embed_table,
    row_ids,
    row_owner,
    lengths,
    feature_slot,
    labels,
    norm_gain,
    cross_weight,
    cross_bias,
    deep_weight,
    deep_bias,
    out_weight,
):
    packed = index_call(
        row_ids.reshape(IDROWS, LANES),
        row_owner.reshape(IDROWS, LANES),
        lengths.reshape(8, 128),
        feature_slot.reshape(KEYS, 1),
    )
    asked = lax.all_to_all(
        packed.reshape(OWNERS, 4, 128), "shard", split_axis=0, concat_axis=0, tiled=True
    )
    rows = ((asked >> 10) & (ROWS - 1)).reshape(-1)
    picked = gather_call(rows, embed_table)
    got = lax.all_to_all(picked, "shard", split_axis=0, concat_axis=0, tiled=True)

    everyone = lax.all_gather(asked, "rep", axis=0, tiled=True).reshape(REPS * OWNERS, CAP)
    rep = lax.axis_index("rep")
    feature = everyone & (FEATS - 1)
    valid = everyone > 0
    within = feature - rep * PAIR
    ours = valid & (within >= 0) & (within < PAIR)
    target = jnp.where(ours, within * VOC + ((everyone >> 10) & (VOC - 1)), PAIR * VOC)
    source = jnp.where(ours, within * SAMPLES + ((everyone >> 3) & (SAMPLES - 1)), 0)
    words = ((target << 8) | source).reshape(-1)
    below = jnp.sum((valid & (within < 0)).astype(I32), axis=1)
    upto = jnp.sum((valid & (within < PAIR)).astype(I32), axis=1)
    first = below // ACCS
    last = (upto + ACCS - 1) // ACCS

    logits, grads, first_local = tower_call(
        got,
        packed,
        labels.reshape(SAMPLES, 1),
        norm_gain.reshape(1, WIDTH),
        cross_weight,
        cross_bias,
        deep_weight,
        deep_bias,
        out_weight.reshape(1, WIDTH),
    )
    mine = lax.all_to_all(grads, "rep", split_axis=0, concat_axis=0, tiled=True)
    all_grads = lax.all_gather(mine, "shard", axis=0)
    part = scatter_call(words, first, last, all_grads)
    blocks = lax.all_gather(part, "rep", axis=0, tiled=True).reshape(FEATS, VOC, EMB)
    slots = feature_slot[lax.axis_index("shard")]
    order = jnp.argmax(
        slots[None, :] == jnp.arange(FEATS, dtype=I32)[:, None], axis=1
    ).astype(I32)
    row_grad = widen_call(order, blocks)
    first_grad = lax.psum(first_local, ("rep", "shard")).astype(F32)
    return (row_grad, first_grad, logits.reshape(SAMPLES))


def solution(mesh):
    both = ("rep", "shard")
    in_specs = (
        P("shard", None),
        P(both, None),
        P(both, None, None),
        P(both, None),
        P(),
        P(both),
        P(),
        P(),
        P(),
        P(),
        P(),
        P(),
    )
    out_specs = (P("shard", None), P(), P(both))
    return jax.shard_map(body, mesh=mesh, in_specs=in_specs, out_specs=out_specs, check_vma=False)
```

time: 1760 us -> 371 us (0.21)
  other arithmetic: 602 us -> 15.1 us
  local copies, waits for them, and re-layouts: 489 us -> 5.04 us
  waiting for transfers between devices: 581 us -> 176 us
  Pallas kernels: 0 us -> 113 us
  blocking collectives: 0 us -> 36.3 us
  matrix products: 29.6 us -> 0 us
  starting transfers between devices: 35.7 us -> 7.86 us
    scatter-add x3 -> x0, other arithmetic: 574 us -> none  [the longest x1 317 us: body(): jax.ops.segment_sum(slot_values.reshape(-1, width).astype(jnp.float32), r...]
    gather x12 -> x0, local copies, waits for them, and re-layouts: 413 us -> none  [the longest x11 362 us: body(): bag_index = jnp.searchsorted(ends, positions, side='right')]
    psum x2 -> x1, waiting for transfers between devices: 407 us -> 91.2 us  [body(): first_grad = lax.psum(first_local, ('rep', 'shard')).astype(F32)]
    pallas_call x0 -> x5, Pallas kernels: none -> 113 us  [the longest x1 34.6 us: tower_call(): pl.pallas_call(tower_kernel, grid=(OWNERS,), in_specs=[pl.BlockSpec((1, C...]
    all_to_all x3 -> x1, waiting for transfers between devices: 112 us -> 48.6 us  [body(): lax.all_to_all(picked, 'shard', split_axis=0, concat_axis=0, tiled=True)]
    scatter x2 -> x0, local copies, waits for them, and re-layouts: 62.1 us -> none  [the longest x1 31 us: body(): bag_send = jnp.full((shards * capacity,), -1, jnp.int32).at[slot].set(bag...]
    dot_general x12 -> x0, matrix products: 29.6 us -> none  [the longest x5 15.2 us: times_transposed(): lax.dot_general(left, right, (((1,), (1,)), ((), ())), preferred_element_...]
    all_to_all x3 -> x1, starting transfers between devices: 35.4 us -> 7.73 us  [body(): lax.all_to_all(picked, 'shard', split_axis=0, concat_axis=0, tiled=True)]
  transfers between devices with their start and end apart: 6 -> 4, of which waited for: 4 -> 3; matrix products, arithmetic and copies ran while one was open for 23% -> 3% of each run, Pallas kernels for 0% -> 7%
where the time goes in v1:
time: 371 us; the launch traced here: 368 us
  waiting for transfers between devices  176 us (47%)
  Pallas kernels  113 us (30%)
  blocking collectives  36.3 us (10%)
  between operations  15.5 us (4%)
  other arithmetic  15.1 us (4%)
  starting transfers between devices  7.86 us (2%)
  local copies, waits for them, and re-layouts  5.04 us (1%)
    psum x1, waiting for transfers between devices, body(): first_grad = lax.psum(first_local, ('rep', 'shard')).astype(F32)  91.2 us
    all_to_all x1, waiting for transfers between devices, body(): lax.all_to_all(picked, 'shard', split_axis=0, concat_axis=0, tiled=True)  48.6 us
    all_gather x1, waiting for transfers between devices, body(): all_grads = lax.all_gather(mine, 'shard', axis=0)  35.2 us
    pallas_call x1, Pallas kernels, tower_call(): pl.pallas_call(tower_kernel, grid=(OWNERS,), in_specs=[pl.BlockSpec((1, C...  34.6 us
    pallas_call x1, Pallas kernels, scatter_call(): pl.pallas_call(scatter_kernel, out_shape=jax.ShapeDtypeStruct((rows, EMB)...  26.2 us
    pallas_call x1, Pallas kernels, gather_call(): pl.pallas_call(gather_kernel, out_shape=jax.ShapeDtypeStruct((OWNERS, CAP...  23.9 us
    pallas_call x1, Pallas kernels, index_call(): pl.pallas_call(index_kernel, out_shape=jax.ShapeDtypeStruct((OWNERS, CAP)...  21.2 us
    all_to_all x1, blocking collectives, body(): lax.all_to_all(packed.reshape(OWNERS, 4, 128), 'shard', split_axis=0, con...  12.5 us
  transfers between devices with their start and end apart: 4, of which 3 were waited for; matrix products, arithmetic and copies ran while one was open for 3% of the time, Pallas kernels for 7%

profile of v1, /device:TPU:38, one launch (start us, length us, event | category | flops | bytes accessed | tf_op | source)
XLA Modules:
  0.0 368.0 jit_solution(18044300874276484111)
XLA Ops:
  8.0 0.8 copy.23
  9.3 1.5 reduce.30
  10.8 0.6 reshape.67.ids_ref
  11.4 1.5 reduce.31
  13.5 0.8 reshape.87.slot_ref
  14.2 21.2 %index.1.packed_ref = s32[32,512]{1,0:T(8,128)} custom-call(s32[32,256]{1,0:T(8,128)} %reshape.67.ids_ref, s32[32,256]{1,0:T(8,128)} %reshape.68.owner_ref, s32[8,128]{1,0:T(8,128)} %bitcast.13, s32[256,1]{1,0:T(8,128)} %reshape.87.slot_ref), custom_call_target="tpu_custom_call" | custom-call | tf_op jit(solution)/shard_map/index/pallas_call | solution.py:122
  35.4 0.9 reshape.71
  36.2 12.5 %all_to_all.15 = s32[32,4,128]{2,1,0:T(4,128)S(1)} all-to-all(s32[32,4,128]{2,1,0:T(4,128)S(1)} %reshape.71), channel_id=1, replica_groups=mesh['rep'=4,'shard'=32] {'shard'}, dimensions={0} | all-to-all | bytes 131072 | tf_op jit(solution)/shard_map/all_to_all | solution.py:415
  48.8 0.6 shift-right-arithmetic_and_fusion
  49.4 23.9 %gather.1 = bf16[32,512,128]{2,1,0:T(8,128)(2,1)} custom-call(s32[16384]{0:T(1024)} %bitcast.12, bf16[8192,128]{1,0:T(8,128)(2,1)} %table_ref.1), custom_call_target="tpu_custom_call" | custom-call | tf_op jit(solution)/shard_map/gather/pallas_call | solution.py:152
  73.3 7.7 %all-to-all-start.1 = ((bf16[32,512,128]{2,1,0:T(8,128)(2,1)}), bf16[32,512,128]{2,1,0:T(8,128)(2,1)}, u32[]{:S(2)}, u32[]{:S(2)}) async-start(bf16[32,512,128]{2,1,0:T(8,128)(2,1)} %gather.1), calls=%async_computation.1 | async-start | bytes 8388608 | tf_op jit(solution)/shard_map/all_to_all | solution.py:420
  81.1 0.7 copy.25.labels_ref
  81.8 48.6 %all-to-all-done.1.got_ref = bf16[32,512,128]{2,1,0:T(8,128)(2,1)} async-done(((bf16[32,512,128]{2,1,0:T(8,128)(2,1)}), bf16[32,512,128]{2,1,0:T(8,128)(2,1)}, u32[]{:S(2)}, u32[]{:S(2)}) %all-to-all-start.1) | async-done | bytes 4194336 | tf_op jit(solution)/shard_map/all_to_all | solution.py:420
  130.4 34.6 %tower.1 = (f32[128,1]{1,0:T(8,128)}, bf16[4,128,256]{2,1,0:T(8,128)(2,1)}, bf16[1024,1024]{1,0:T(8,128)(2,1)}) custom-call(bf16[32,512,128]{2,1,0:T(8,128)(2,1)} %all-to-all-done.1.got_ref, s32[32,512]{1,0:T(8,128)} %index.1.packed_ref, s32[128,1]{1,0:T(8,128)} %copy.25.labels_ref, f32[1,1024]{1,0:T(1,128)} %bitcast.14, f32[3,1024]{1,0:T(4,128)} %cbias_ref.1, ...), custom_call_target="tpu_custom_call" | custom-call | tf_op jit(solution)/shard_map/tower/pallas_call | solution.py:270
  165.0 11.3 %all_to_all.16 = bf16[4,128,256]{2,1,0:T(8,128)(2,1)} all-to-all(bf16[4,128,256]{2,1,0:T(8,128)(2,1)} %get-tuple-element.8), channel_id=1, replica_groups=mesh['rep'=4,'shard'=32] {'rep'}, dimensions={0} | all-to-all | bytes 524288 | tf_op jit(solution)/shard_map/all_to_all | solution.py:447
  177.0 12.4 %all_gather.12 = s32[128,4,128]{2,1,0:T(4,128)S(1)} all-gather(s32[32,4,128]{2,1,0:T(4,128)S(1)} %all_to_all.15), channel_id=1, replica_groups=mesh['rep'=4,'shard'=32] {'rep'}, dimensions={0}, use_global_device_ids=true | all-gather | bytes 327680 | tf_op jit(solution)/shard_map/all_gather | solution.py:422
  189.5 5.6 %convert_reduce_fusion = (s32[128]{0:T(128)S(1)}, s32[128]{0:T(128)S(1)}, s32[128,4,128]{2,1,0:T(4,128)}) fusion(s32[128,4,128]{2,1,0:T(4,128)S(1)} %all_gather.12, s32[]{:T(128)S(6)} %mul.19), kind=kLoop, calls=%fused_computation.1 | loop fusion | flops 1703680 | bytes 525316 | tf_op jit(solution)/shard_map/reduce_sum | solution.py:432
  195.6 35.2 %all-gather.6.cloned.1.call-done = bf16[128,128,256]{2,1,0:T(8,128)(2,1)} async-done(((bf16[4,128,256]{2,1,0:T(8,128)(2,1)}), bf16[128,128,256]{2,1,0:T(8,128)(2,1)}) %all-gather.6.cloned.1.call-update) | async-done | bytes 8388624 | tf_op jit(solution)/shard_map/all_gather | solution.py:448
  230.7 26.2 %scatter.1 = bf16[2048,128]{1,0:T(8,128)(2,1)} custom-call(s32[65536]{0:T(1024)} %bitcast.11, s32[128]{0:T(128)} %get-tuple-element.15.first_ref, s32[128]{0:T(128)} %get-tuple-element.14.last_ref, bf16[32,4,128,256]{3,2,1,0:T(8,128)(2,1)} %bitcast.9), custom_call_target="tpu_custom_call" | custom-call | tf_op jit(solution)/shard_map/scatter/pallas_call | solution.py:356
  257.2 0.7 iota_reduce_fusion
  257.9 0.6 reduce.23
  258.5 91.2 %all-reduce.2.cloned.1.call-done = bf16[1024,1024]{1,0:T(8,128)(2,1)} async-done(((bf16[1024,1024]{1,0:T(8,128)(2,1)}), bf16[1024,1024]{1,0:T(8,128)(2,1)}) %all-reduce.2.cloned.1.call-update) | async-done | bytes 2097168 | tf_op jit(solution)/shard_map/psum | solution.py:456
  349.8 4.1 %convert_element_type.13 = f32[1024,1024]{1,0:T(8,128)} convert(bf16[1024,1024]{1,0:T(8,128)(2,1)} %all-reduce.2.cloned.1.call-done) | non-fusion elementwise | flops 1048576 | bytes 6291456 | tf_op jit(solution)/shard_map/convert_element_type | solution.py:456
  353.9 6.7 %widen.1 = f32[8192,128]{1,0:T(8,128)} custom-call(s32[8]{0:T(128)} %get-tuple-element.7.order_ref, bf16[8,1024,128]{2,1,0:T(8,128)(2,1)} %bitcast.10), custom_call_target="tpu_custom_call" | custom-call | tf_op jit(solution)/shard_map/widen/pallas_call | solution.py:382
  (17 shorter events, 2.5 us)
Async XLA Ops:
  73.3 7.8 %copy-start.2 = (s32[128]{0:T(128)S(1)}, s32[128]{0:T(128)}, u32[]{:S(2)}) copy-start(s32[128]{0:T(128)} %param.17) | copy-start | bytes 1540
  73.3 57.1 %all-to-all-start.1 = ((bf16[32,512,128]{2,1,0:T(8,128)(2,1)}), bf16[32,512,128]{2,1,0:T(8,128)(2,1)}, u32[]{:S(2)}, u32[]{:S(2)}) async-start(bf16[32,512,128]{2,1,0:T(8,128)(2,1)} %gather.1), calls=%async_computation.1 | async-start | bytes 8388608 | tf_op jit(solution)/shard_map/all_to_all | solution.py:420
  81.1 149.7 %all-gather.6.cloned.1.call-start = ((), (), s32[]{:S(2)}) async-start(), calls=%async_computation.5 | async-start | bytes 8650752 | tf_op jit(solution)/shard_map/all_gather | solution.py:448
  176.4 173.4 %all-reduce.2.cloned.1.call-start = ((), (), s32[]{:S(2)}) async-start(), calls=%async_computation.4 | async-start | bytes 4194304 | tf_op jit(solution)/shard_map/psum | solution.py:456
  177.0 176.9 %all-gather.4.cloned.1.call-start = ((), (), s32[]{:S(2)}) async-start(), calls=%async_computation.3 | async-start | bytes 2621440 | tf_op jit(solution)/shard_map/all_gather | solution.py:450
  230.7 26.3 %copy-start.1 = (s32[32,8]{0,1:T(8,128)S(1)}, s32[32,8]{0,1:T(8,128)}, u32[]{:S(2)}) copy-start(s32[32,8]{0,1:T(8,128)} %param.16) | copy-start | bytes 3076
  230.7 27.2 %copy-start = (f32[128,1]{1,0:T(8,128)S(1)}, f32[128,1]{1,0:T(8,128)}, u32[]{:S(2)}) copy-start(f32[128,1]{1,0:T(8,128)} %get-tuple-element.10) | copy-start | bytes 1540
Sparse Core Ops, SparseCore 0:
  176.5 54.1 all-gather.5
  257.1 63.5 all-gather.3
Sparse Core Ops, SparseCore 1:
  182.3 167.4 all-reduce.1

commit v2 on v1

--- a/solution.py
+++ b/solution.py
@@ -251,7 +251,9 @@
             gx_ref[...] += grad * cross_t[layer]
             grad = grad + dot(crossed, cross_w[layer], NT)
             if layer == 0:
-                first_ref[...] = dot(start_ref[...], crossed, TN).astype(first_ref.dtype)
+                summed = dot(start_ref[...], crossed, TN).reshape(OWNERS, REPS, 8, WIDTH)
+                for r in range(REPS):
+                    first_ref[r] = summed[:, r].reshape(OWNERS * 8, WIDTH).astype(BF)
         scaled = (gx_ref[...] + grad) * gain
         pooled = jnp.concatenate(
             [pooled_ref[f * SAMPLES : (f + 1) * SAMPLES, :] for f in range(FEATS)], axis=1
@@ -284,12 +286,12 @@
         out_specs=[
             whole((SAMPLES, 1)),
             whole((REPS, SAMPLES, PAIR * EMB)),
-            whole((WIDTH, WIDTH)),
+            whole((REPS, OWNERS * 8, WIDTH)),
         ],
         out_shape=[
             jax.ShapeDtypeStruct((SAMPLES, 1), F32),
             jax.ShapeDtypeStruct((REPS, SAMPLES, PAIR * EMB), BF),
-            jax.ShapeDtypeStruct((WIDTH, WIDTH), BF),
+            jax.ShapeDtypeStruct((REPS, OWNERS * 8, WIDTH), BF),
         ],
         scratch_shapes=[
             pltpu.VMEM((BAGS, EMB), F32),
@@ -373,23 +375,48 @@
     )(words, first, last, grads)
 
 
-def widen_kernel(order_ref, in_ref, out_ref):
-    del order_ref
-    out_ref[...] = in_ref[0].astype(F32)
-
-
-def widen_call(order, blocks):
+def finish_kernel(order_ref, *refs):
+    parts, first_ref, rows_ref, grad_ref = refs[:REPS], refs[REPS], refs[REPS + 1], refs[REPS + 2]
+    source = order_ref[pl.program_id(0)]
+    for k in range(REPS):
+
+        @pl.when(source // PAIR == k)
+        def _():
+            rows_ref[...] = parts[k][lax.rem(source, PAIR)].astype(F32)
+
+    grad_ref[...] = first_ref[...].astype(F32)
+
+
+def finish_call(order, parts, first):
+    rows = WIDTH // FEATS
     return pl.pallas_call(
-        widen_kernel,
-        out_shape=jax.ShapeDtypeStruct((ROWS, EMB), F32),
+        finish_kernel,
+        out_shape=[
+            jax.ShapeDtypeStruct((ROWS, EMB), F32),
+            jax.ShapeDtypeStruct((WIDTH, WIDTH), F32),
+        ],
         grid_spec=pltpu.PrefetchScalarGridSpec(
             num_scalar_prefetch=1,
             grid=(FEATS,),
-            in_specs=[pl.BlockSpec((1, VOC, EMB), lambda i, o: (o[i], 0, 0))],
-            out_specs=pl.BlockSpec((VOC, EMB), lambda i, o: (i, 0)),
+            in_specs=[pl.BlockSpec((PAIR, VOC, EMB), lambda i, o: (0, 0, 0)) for _ in parts]
+            + [pl.BlockSpec((rows, WIDTH), lambda i, o: (i, 0))],
+            out_specs=[
+                pl.BlockSpec((VOC, EMB), lambda i, o: (i, 0)),
+                pl.BlockSpec((rows, WIDTH), lambda i, o: (i, 0)),
+            ],
         ),
-        name="widen",
-    )(order, blocks)
+        compiler_params=pltpu.CompilerParams(vmem_limit_bytes=VMEM),
+        name="finish",
+    )(order, *parts, first)
+
+
+def from_before(x, axis, k):
+    n = lax.axis_size(axis)
+    return lax.ppermute(x, axis, [(i, (i + k) % n) for i in range(n)])
+
+
+def summed(x):
+    return jnp.sum(x.astype(F32), axis=0).astype(BF)
 
 
 def body(
@@ -430,8 +457,8 @@
     words = ((target << 8) | source).reshape(-1)
     below = jnp.sum((valid & (within < 0)).astype(I32), axis=1)
     upto = jnp.sum((valid & (within < PAIR)).astype(I32), axis=1)
-    first = below // ACCS
-    last = (upto + ACCS - 1) // ACCS
+    first_block = below // ACCS
+    last_block = (upto + ACCS - 1) // ACCS
 
     logits, grads, first_local = tower_call(
         got,
@@ -445,15 +472,28 @@
         out_weight.reshape(1, WIDTH),
     )
     mine = lax.all_to_all(grads, "rep", split_axis=0, concat_axis=0, tiled=True)
+    mine, first_local = lax.optimization_barrier((mine, first_local))
     all_grads = lax.all_gather(mine, "shard", axis=0)
-    part = scatter_call(words, first, last, all_grads)
-    blocks = lax.all_gather(part, "rep", axis=0, tiled=True).reshape(FEATS, VOC, EMB)
+    quarter = summed(
+        lax.all_to_all(first_local, "rep", split_axis=0, concat_axis=0, tiled=True)
+    )
+    eight = summed(
+        lax.all_to_all(
+            quarter.reshape(OWNERS, 8, WIDTH), "shard", split_axis=0, concat_axis=0, tiled=True
+        )
+    )
+    first = lax.all_gather(
+        lax.all_gather(eight, "rep", axis=0, tiled=True), "shard", axis=0, tiled=True
+    )
+
+    part = scatter_call(words, first_block, last_block, all_grads).reshape(PAIR, VOC, EMB)
+    parts = [part] + [from_before(part, "rep", k) for k in range(1, REPS)]
     slots = feature_slot[lax.axis_index("shard")]
-    order = jnp.argmax(
+    feature_of = jnp.argmax(
         slots[None, :] == jnp.arange(FEATS, dtype=I32)[:, None], axis=1
     ).astype(I32)
-    row_grad = widen_call(order, blocks)
-    first_grad = lax.psum(first_local, ("rep", "shard")).astype(F32)
+    order = ((rep - feature_of // PAIR) & (REPS - 1)) * PAIR + feature_of % PAIR
+    row_grad, first_grad = finish_call(order, parts, first)
     return (row_grad, first_grad, logits.reshape(SAMPLES))
 
 

time: 371 us -> 353 us (0.951)
  waiting for transfers between devices: 176 us -> 60.5 us
  blocking collectives: 36.3 us -> 101 us
  Pallas kernels: 113 us -> 144 us
  starting transfers between devices: 7.86 us -> 12.5 us
    psum x1 -> x0, waiting for transfers between devices: 91.2 us -> none  [body(): first_grad = lax.psum(first_local, ('rep', 'shard')).astype(F32)]
    all_to_all x0 -> x2, blocking collectives: none -> 52.4 us  [the longest x1 28.8 us: body(): lax.all_to_all(first_local, 'rep', split_axis=0, concat_axis=0, tiled=True)]
    all_gather x1, waiting for transfers between devices: 35.2 us -> 0.01 us  [body(): all_grads = lax.all_gather(mine, 'shard', axis=0)]
    pallas_call x1, Pallas kernels: 26.2 us -> 56.2 us  [scatter_call(): pl.pallas_call(scatter_kernel, out_shape=jax.ShapeDtypeStruct((rows, EMB)...]
    all_gather x0 -> x1, blocking collectives: none -> 12.6 us  [body(): lax.all_gather(eight, 'rep', axis=0, tiled=True)]
    ppermute x0 -> x3, waiting for transfers between devices: none -> 11.9 us  [from_before(): return lax.ppermute(x, axis, [(i, (i + k) % n) for i in range(n)])]
    ppermute x0 -> x3, starting transfers between devices: none -> 4.72 us  [from_before(): return lax.ppermute(x, axis, [(i, (i + k) % n) for i in range(n)])]
    convert_element_type x1 -> x0, other arithmetic: 4.07 us -> none  [body(): first_grad = lax.psum(first_local, ('rep', 'shard')).astype(F32)]
  transfers between devices with their start and end apart: 4 -> 6, of which waited for: 3 -> 3; matrix products, arithmetic and copies ran while one was open for 3% -> 3% of each run, Pallas kernels for 7% -> 16%
where the time goes in v2:
time: 353 us; the launch traced here: 350 us
  Pallas kernels  144 us (41%)
  blocking collectives  101 us (29%)
  waiting for transfers between devices  60.5 us (17%)
  between operations  14.1 us (4%)
  starting transfers between devices  12.5 us (4%)
  other arithmetic  12 us (3%)
  local copies, waits for them, and re-layouts  5.84 us (2%)
    pallas_call x1, Pallas kernels, scatter_call(): pl.pallas_call(scatter_kernel, out_shape=jax.ShapeDtypeStruct((rows, EMB)...  56.2 us
    all_to_all x1, waiting for transfers between devices, body(): lax.all_to_all(picked, 'shard', split_axis=0, concat_axis=0, tiled=True)  48.6 us
    pallas_call x1, Pallas kernels, tower_call(): pl.pallas_call(tower_kernel, grid=(OWNERS,), in_specs=[pl.BlockSpec((1, C...  34.6 us
    all_to_all x1, blocking collectives, body(): lax.all_to_all(first_local, 'rep', split_axis=0, concat_axis=0, tiled=True)  28.8 us
    pallas_call x1, Pallas kernels, gather_call(): pl.pallas_call(gather_kernel, out_shape=jax.ShapeDtypeStruct((OWNERS, CAP...  23.9 us
    all_to_all x1, blocking collectives, body(): lax.all_to_all(quarter.reshape(OWNERS, 8, WIDTH), 'shard', split_axis=0,...  23.6 us
    pallas_call x1, Pallas kernels, index_call(): pl.pallas_call(index_kernel, out_shape=jax.ShapeDtypeStruct((OWNERS, CAP)...  21.2 us
    all_gather x1, blocking collectives, body(): lax.all_gather(eight, 'rep', axis=0, tiled=True)  12.6 us
  transfers between devices with their start and end apart: 6, of which 3 were waited for; matrix products, arithmetic and copies ran while one was open for 3% of the time, Pallas kernels for 16%

profile of v2, /device:TPU:38, one launch (start us, length us, event | category | flops | bytes accessed | tf_op | source)
XLA Modules:
  0.0 350.0 jit_solution(4256530221322873809)
XLA Ops:
  7.2 0.8 copy.23
  8.4 1.5 reduce.32
  10.5 1.5 reduce.33
  13.4 21.2 %index.1.packed_ref = s32[32,512]{1,0:T(8,128)} custom-call(s32[32,256]{1,0:T(8,128)} %reshape.70.ids_ref, s32[32,256]{1,0:T(8,128)} %reshape.71.owner_ref, s32[8,128]{1,0:T(8,128)} %bitcast.18, s32[256,1]{1,0:T(8,128)} %reshape.91.slot_ref), custom_call_target="tpu_custom_call" | custom-call | tf_op jit(solution)/shard_map/index/pallas_call | solution.py:122
  34.5 0.9 reshape.74
  35.4 12.5 %all_to_all.25 = s32[32,4,128]{2,1,0:T(4,128)S(1)} all-to-all(s32[32,4,128]{2,1,0:T(4,128)S(1)} %reshape.74), channel_id=1, replica_groups=mesh['rep'=4,'shard'=32] {'shard'}, dimensions={0} | all-to-all | bytes 131072 | tf_op jit(solution)/shard_map/all_to_all | solution.py:442
  48.6 23.9 %gather.1 = bf16[32,512,128]{2,1,0:T(8,128)(2,1)} custom-call(s32[16384]{0:T(1024)} %bitcast.17, bf16[8192,128]{1,0:T(8,128)(2,1)} %table_ref.1), custom_call_target="tpu_custom_call" | custom-call | tf_op jit(solution)/shard_map/gather/pallas_call | solution.py:152
  72.5 7.7 %all-to-all-start.1 = ((bf16[32,512,128]{2,1,0:T(8,128)(2,1)}), bf16[32,512,128]{2,1,0:T(8,128)(2,1)}, u32[]{:S(2)}, u32[]{:S(2)}) async-start(bf16[32,512,128]{2,1,0:T(8,128)(2,1)} %gather.1), calls=%async_computation.1 | async-start | bytes 8388608 | tf_op jit(solution)/shard_map/all_to_all | solution.py:447
  81.0 48.6 %all-to-all-done.1.got_ref = bf16[32,512,128]{2,1,0:T(8,128)(2,1)} async-done(((bf16[32,512,128]{2,1,0:T(8,128)(2,1)}), bf16[32,512,128]{2,1,0:T(8,128)(2,1)}, u32[]{:S(2)}, u32[]{:S(2)}) %all-to-all-start.1) | async-done | bytes 4194336 | tf_op jit(solution)/shard_map/all_to_all | solution.py:447
  129.6 34.6 %tower.1 = (f32[128,1]{1,0:T(8,128)}, bf16[4,128,256]{2,1,0:T(8,128)(2,1)}, bf16[4,256,1024]{2,1,0:T(8,128)(2,1)}) custom-call(bf16[32,512,128]{2,1,0:T(8,128)(2,1)} %all-to-all-done.1.got_ref, s32[32,512]{1,0:T(8,128)} %index.1.packed_ref, s32[128,1]{1,0:T(8,128)} %copy.25.labels_ref, f32[1,1024]{1,0:T(1,128)} %bitcast.19, f32[3,1024]{1,0:T(4,128)} %cbias_ref.1, ...), custom_call_target="tpu_custom_call" | custom-call | tf_op jit(solution)/shard_map/tower/pallas_call | solution.py:272
  164.2 11.3 %all_to_all.26 = bf16[4,128,256]{2,1,0:T(8,128)(2,1)} all-to-all(bf16[4,128,256]{2,1,0:T(8,128)(2,1)} %get-tuple-element.12), channel_id=1, replica_groups=mesh['rep'=4,'shard'=32] {'rep'}, dimensions={0} | all-to-all | bytes 524288 | tf_op jit(solution)/shard_map/all_to_all | solution.py:474
  175.6 28.8 %all_to_all.27 = bf16[4,256,1024]{2,1,0:T(8,128)(2,1)S(1)} all-to-all(bf16[4,256,1024]{2,1,0:T(8,128)(2,1)} %get-tuple-element.15), channel_id=1, replica_groups=mesh['rep'=4,'shard'=32] {'rep'}, dimensions={0} | all-to-all | bytes 4194304 | tf_op jit(solution)/shard_map/all_to_all | solution.py:478
  204.8 23.6 %all_to_all.28 = bf16[32,8,1024]{2,1,0:T(8,128)(2,1)S(1)} all-to-all(bf16[32,8,1024]{2,1,0:T(8,128)(2,1)S(1)} %bitcast.15), channel_id=1, replica_groups=mesh['rep'=4,'shard'=32] {'shard'}, dimensions={0} | all-to-all | bytes 1048576 | tf_op jit(solution)/shard_map/all_to_all | solution.py:481
  228.4 12.6 %all_gather.18 = bf16[32,1024]{1,0:T(8,128)(2,1)} all-gather(bf16[8,1024]{1,0:T(8,128)(2,1)S(1)} %reduce_sum.45), channel_id=1, replica_groups=mesh['rep'=4,'shard'=32] {'rep'}, dimensions={0}, use_global_device_ids=true | all-gather | bytes 81920 | tf_op jit(solution)/shard_map/all_gather | solution.py:486
  241.1 12.4 %all_gather.15 = s32[128,4,128]{2,1,0:T(4,128)S(1)} all-gather(s32[32,4,128]{2,1,0:T(4,128)S(1)} %all_to_all.25), channel_id=1, replica_groups=mesh['rep'=4,'shard'=32] {'rep'}, dimensions={0}, use_global_device_ids=true | all-gather | bytes 327680 | tf_op jit(solution)/shard_map/all_gather | solution.py:449
  253.5 5.5 %convert_reduce_fusion = (s32[128]{0:T(128)S(1)}, s32[128]{0:T(128)S(1)}, s32[128,4,128]{2,1,0:T(4,128)}) fusion(s32[128,4,128]{2,1,0:T(4,128)S(1)} %all_gather.15, s32[]{:T(128)S(6)} %mul.23), kind=kLoop, calls=%fused_computation.1 | loop fusion | flops 1703680 | bytes 525316 | tf_op jit(solution)/shard_map/reduce_sum | solution.py:459
  259.6 56.2 %scatter.1 = bf16[2048,128]{1,0:T(8,128)(2,1)} custom-call(s32[65536]{0:T(1024)} %bitcast.16, s32[128]{0:T(128)} %get-tuple-element.23.first_ref, s32[128]{0:T(128)} %get-tuple-element.22.last_ref, bf16[32,4,128,256]{3,2,1,0:T(8,128)(2,1)} %bitcast.10), custom_call_target="tpu_custom_call" | custom-call | tf_op jit(solution)/shard_map/scatter/pallas_call | solution.py:358
  315.8 2.1 collective-permute-start.2
  317.9 1.6 collective-permute-start.1
  319.5 1.0 collective-permute-start
  322.5 8.1 %collective-permute-done.2.refs_3_ = bf16[2,1024,128]{2,1,0:T(8,128)(2,1)S(1)} collective-permute-done((bf16[2,1024,128]{2,1,0:T(8,128)(2,1)}, bf16[2,1024,128]{2,1,0:T(8,128)(2,1)S(1)}, u32[]{:S(2)}, u32[]{:S(2)}) %collective-permute-start.2) | collective-permute-done | bytes 524320 | tf_op jit(solution)/shard_map/ppermute | solution.py:415
  330.6 3.8 %collective-permute-done.refs_1_ = bf16[2,1024,128]{2,1,0:T(8,128)(2,1)S(1)} collective-permute-done((bf16[2,1024,128]{2,1,0:T(8,128)(2,1)}, bf16[2,1024,128]{2,1,0:T(8,128)(2,1)S(1)}, u32[]{:S(2)}, u32[]{:S(2)}) %collective-permute-start) | collective-permute-done | bytes 524320 | tf_op jit(solution)/shard_map/ppermute | solution.py:415
  334.4 0.8 copy-done.2
  335.2 8.0 %finish.1 = (f32[8192,128]{1,0:T(8,128)}, f32[1024,1024]{1,0:T(8,128)}) custom-call(s32[8]{0:T(128)} %fusion.1.order_ref, bf16[2,1024,128]{2,1,0:T(8,128)(2,1)} %bitcast.14, bf16[2,1024,128]{2,1,0:T(8,128)(2,1)} %copy-done.2, bf16[2,1024,128]{2,1,0:T(8,128)(2,1)} %copy-done.1, bf16[2,1024,128]{2,1,0:T(8,128)(2,1)} %copy-done, ...), custom_call_target="tpu_custom_call" | custom-call | tf_op jit(solution)/shard_map/finish/pallas_call | solution.py:392
  (31 shorter events, 7.0 us)
Async XLA Ops:
  72.5 7.8 %copy-start.5 = (s32[128]{0:T(128)S(1)}, s32[128]{0:T(128)}, u32[]{:S(2)}) copy-start(s32[128]{0:T(128)} %param.17) | copy-start | bytes 1540
  72.5 57.1 %all-to-all-start.1 = ((bf16[32,512,128]{2,1,0:T(8,128)(2,1)}), bf16[32,512,128]{2,1,0:T(8,128)(2,1)}, u32[]{:S(2)}, u32[]{:S(2)}) async-start(bf16[32,512,128]{2,1,0:T(8,128)(2,1)} %gather.1), calls=%async_computation.1 | async-start | bytes 8388608 | tf_op jit(solution)/shard_map/all_to_all | solution.py:447
  80.2 179.3 %all-gather.6.cloned.1.call-start = ((), (), s32[]{:S(2)}) async-start(), calls=%async_computation.6 | async-start | bytes 8650752 | tf_op jit(solution)/shard_map/all_gather | solution.py:476
  175.5 147.0 %all-gather.4.cloned.1.call-start = ((), (), s32[]{:S(2)}) async-start(), calls=%async_computation.5 | async-start | bytes 2162688 | tf_op jit(solution)/shard_map/all_gather | solution.py:485
  259.6 60.9 %copy-start.4 = (s32[32,8]{0,1:T(8,128)S(1)}, s32[32,8]{0,1:T(8,128)}, u32[]{:S(2)}) copy-start(s32[32,8]{0,1:T(8,128)} %param.16) | copy-start | bytes 3076
  259.6 62.3 %copy-start.3 = (f32[128,1]{1,0:T(8,128)S(1)}, f32[128,1]{1,0:T(8,128)}, u32[]{:S(2)}) copy-start(f32[128,1]{1,0:T(8,128)} %get-tuple-element.18) | copy-start | bytes 1540
  315.8 14.8 %collective-permute-start.2 = (bf16[2,1024,128]{2,1,0:T(8,128)(2,1)}, bf16[2,1024,128]{2,1,0:T(8,128)(2,1)S(1)}, u32[]{:S(2)}, u32[]{:S(2)}) collective-permute-start(bf16[2,1024,128]{2,1,0:T(8,128)(2,1)} %bitcast.11), channel_id=1, source_target_pairs={{0,96},{32,0},{64,32},{96,64},{1,97},{33,1},{65,33},{97,65},{2,98}... | collective-permute-start | bytes 1572872 | tf_op jit(solution)/shard_map/ppermute | solution.py:415
  317.9 12.7 %collective-permute-start.1 = (bf16[2,1024,128]{2,1,0:T(8,128)(2,1)}, bf16[2,1024,128]{2,1,0:T(8,128)(2,1)S(1)}, u32[]{:S(2)}, u32[]{:S(2)}) collective-permute-start(bf16[2,1024,128]{2,1,0:T(8,128)(2,1)} %bitcast.12), channel_id=1, source_target_pairs={{0,64},{32,96},{64,0},{96,32},{1,65},{33,97},{65,1},{97,33},{2,66}... | collective-permute-start | bytes 1572872 | tf_op jit(solution)/shard_map/ppermute | solution.py:415
  319.5 14.9 %collective-permute-start = (bf16[2,1024,128]{2,1,0:T(8,128)(2,1)}, bf16[2,1024,128]{2,1,0:T(8,128)(2,1)S(1)}, u32[]{:S(2)}, u32[]{:S(2)}) collective-permute-start(bf16[2,1024,128]{2,1,0:T(8,128)(2,1)} %bitcast.13), channel_id=1, source_target_pairs={{0,32},{32,64},{64,96},{96,0},{1,33},{33,65},{65,97},{97,1},{2,34}... | collective-permute-start | bytes 1572872 | tf_op jit(solution)/shard_map/ppermute | solution.py:415
  330.6 3.9 %copy-start = (bf16[2,1024,128]{2,1,0:T(8,128)(2,1)}, bf16[2,1024,128]{2,1,0:T(8,128)(2,1)S(1)}, u32[]{:S(2)}) copy-start(bf16[2,1024,128]{2,1,0:T(8,128)(2,1)S(1)} %collective-permute-done.2.refs_3_) | copy-start | bytes 1572868
  330.6 3.8 %copy-start.1 = (bf16[2,1024,128]{2,1,0:T(8,128)(2,1)}, bf16[2,1024,128]{2,1,0:T(8,128)(2,1)S(1)}, u32[]{:S(2)}) copy-start(bf16[2,1024,128]{2,1,0:T(8,128)(2,1)S(1)} %collective-permute-done.1.refs_2_) | copy-start | bytes 1572868
  334.4 0.8 copy-start.2
Sparse Core Ops, SparseCore 0:
  175.6 58.9 all-gather.5
  241.2 41.4 all-gather.3
